TPU v7x, 32 devices: a whole 2x2x4 slice. The times are simulated.
32 devices in a mesh: dp: 8 (over y, x, core), tensor: 4 (over z).
Axes of the slice: x: 2, y: 2, z: 4, core: 2. Of those that a mesh axis runs over, the one named last changes fastest.
Arguments:
- tokens: bfloat16 [3072, 2048], P('dp'), may hold values from -6 to 6
- out_grad: bfloat16 [3072, 7168], P('dp', 'tensor'), may hold values from -6 to 6
- gate_weight: bfloat16 [2048, 7168], P('dp', 'tensor'), may hold values from -0.1875 to 0.1875
- up_weight: bfloat16 [2048, 7168], P('dp', 'tensor'), may hold values from -0.1875 to 0.1875
- gate_mask: int32 [32, 112], P('dp', 'tensor'), may hold values 0 or 1
- up_mask: int32 [32, 112], P('dp', 'tensor'), may hold values 0 or 1
Outputs:
- hidden: float32 [3072, 7168], P('dp', 'tensor')
- grad_tokens: bfloat16 [3072, 2048], P('dp')
- grad_gate: float32 [2048, 7168], P('dp', 'tensor')
- grad_up: float32 [2048, 7168], P('dp', 'tensor')
All inputs are finite; a program needn't handle non-finite values. No bound on the sum of `gate_mask` or of `up_mask` on one device may be relied on, other than what follows from the above.
Results may differ from a plain program's by a relative error of at most 0.014.
Values may be sent and summed in bfloat16 or wider, within the bound.
A program may use at most 128 MiB of HBM per device.

v0:
```python
import jax
import jax.numpy as jnp
from jax import lax
from jax.sharding import PartitionSpec as P

BLOCK = 64


def expand(block_mask):
    height, breadth = block_mask.shape
    values = block_mask.astype(jnp.float32)
    return jnp.broadcast_to(values[:, None, :, None], (height, BLOCK, breadth, BLOCK)).reshape(
        height * BLOCK, breadth * BLOCK
    )


def local(tokens, out_grad, gate_weight, up_weight, gate_mask, up_mask):
    gate_keep = expand(gate_mask)
    up_keep = expand(up_mask)
    gate_eff = gate_weight * gate_keep.astype(jnp.bfloat16)
    up_eff = up_weight * up_keep.astype(jnp.bfloat16)
    local_both = jnp.concatenate([gate_eff, up_eff], axis=1)
    hidden_width = gate_weight.shape[1]
    gathered = lax.all_gather(local_both, "dp", axis=0, tiled=True)
    preact = jnp.dot(tokens, gathered, preferred_element_type=jnp.float32)
    gate = preact[:, :hidden_width]
    up = preact[:, hidden_width:]
    sigmoid_gate = jax.nn.sigmoid(gate)
    activation = gate * sigmoid_gate
    hidden = activation * up
    grad_float = out_grad.astype(jnp.float32)
    d_gate = (grad_float * up * sigmoid_gate * (1.0 + gate * (1.0 - sigmoid_gate))).astype(
        jnp.bfloat16
    )
    d_up = (grad_float * activation).astype(jnp.bfloat16)
    d_both = jnp.concatenate([d_gate, d_up], axis=1)
    partial_input = lax.dot_general(
        d_both, gathered, (((1,), (1,)), ((), ())), preferred_element_type=jnp.float32
    )
    grad_tokens = lax.psum(partial_input, "tensor").astype(jnp.bfloat16)
    summed = lax.psum_scatter(
        lax.dot_general(
            tokens, d_both, (((0,), (0,)), ((), ())), preferred_element_type=jnp.float32
        ).astype(jnp.bfloat16),
        "dp",
        scatter_dimension=0,
        tiled=True,
    ).astype(jnp.float32)
    grad_gate = summed[:, :hidden_width] * gate_keep
    grad_up = summed[:, hidden_width:] * up_keep
    return (hidden, grad_tokens, grad_gate, grad_up)


def solution(mesh):
    placed = (
        P("dp", None),
        P("dp", "tensor"),
        P("dp", "tensor"),
        P("dp", "tensor"),
        P("dp", "tensor"),
        P("dp", "tensor"),
    )
    return jax.shard_map(
        local,
        mesh=mesh,
        in_specs=placed,
        out_specs=(P("dp", "tensor"), P("dp", None), P("dp", "tensor"), P("dp", "tensor")),
        check_vma=False,
    )
```

profile of v0, /device:TPU:8, one launch (start us, length us, event | category | flops | bytes accessed | tf_op | source)
XLA Modules:
  0.0 285.6 jit_solution(8473674529965623266)
XLA Ops:
  7.2 0.0 copy-start
  7.2 0.0 all-gather.2.cloned.1.call-start
  7.2 0.8 convert_element_type.33
  8.0 0.7 convert_element_type.35
  8.7 0.1 copy.12
  8.8 0.1 copy.10
  8.9 2.2 copy.11
  11.1 2.2 copy.13
  13.3 2.3 broadcast_in_dim.4
  15.7 3.7 %reshape.16 = f32[256,1792]{0,1:T(8,128)S(1)} reshape(f32[4,64,28,64]{1,0,3,2:T(4,128)} %broadcast_in_dim.4) | data formatting | bytes 3670016 | tf_op jit(solution)/shard_map/reshape | solution.py:12
  19.4 2.3 broadcast_in_dim.5
  21.7 4.7 %reshape.17 = f32[256,1792]{0,1:T(8,128)} reshape(f32[4,64,28,64]{1,0,3,2:T(4,128)} %broadcast_in_dim.5) | data formatting | bytes 3670016 | tf_op jit(solution)/shard_map/reshape | solution.py:12
  26.4 2.3 convert_multiply_fusion.2
  28.7 1.3 pad_maximum_fusion.1
  30.1 0.0 all-gather.2.cloned.1.call-update
  30.1 0.2 reduce-scatter.2.cloned.1.call-start
  30.3 2.5 copy.14
  32.8 82.4 %all-gather.2.cloned.1.call-done = bf16[2048,3584]{0,1:T(8,128)(2,1)} async-done(((bf16[256,3584]{0,1:T(8,128)(2,1)}), bf16[2048,3584]{0,1:T(8,128)(2,1)}) %all-gather.2.cloned.1.call-update) | async-done | bytes 14680080 | tf_op jit(solution)/shard_map/all_gather | solution.py:24
  115.2 0.0 copy-done
  115.2 0.0 copy-start.4
  115.2 10.8 %convolution_bitcast_fusion = f32[384,3584]{0,1:T(8,128)S(1)} fusion(bf16[2048,3584]{0,1:T(8,128)(2,1)} %all-gather.2.cloned.1.call-done, bf16[384,2048]{1,0:T(8,128)(2,1)S(1)} %copy-done), kind=kOutput, calls=%fused_computation.2 | convolution fusion | flops 5637144576 | bytes 21757952 | tf_op jit(solution)/shard_map/dot_general | solution.py:25
  126.1 0.0 copy-done.4
  126.1 3.2 %fusion.3 = (bf16[384,1792]{0,1:T(8,128)(2,1)S(1)}, bf16[384,1792]{0,1:T(8,128)(2,1)S(1)}, f32[384,1792]{0,1:T(8,128)}) fusion(bf16[384,1792]{0,1:T(8,128)(2,1)S(1)} %copy-done.4, f32[384,3584]{0,1:T(8,128)S(1)} %convolution_bitcast_fusion), kind=kLoop, calls=%fused_computation.7 | loop fusion | flops 10321920 | bytes 12386304 | tf_op jit(solution)/shard_map/convert_element_type | solution.py:32
  129.3 0.0 copy-start.5
  129.3 0.0 copy-start.7
  129.3 1.1 copy-done.5
  130.4 0.5 copy-done.7
  130.8 13.5 %fusion = bf16[2048,3584]{0,1:T(8,128)(2,1)} fusion(bf16[384,2048]{1,0:T(8,128)(2,1)S(1)} %copy-done, bf16[384,1792]{0,1:T(8,128)(2,1)S(1)} %get-tuple-element.9, bf16[384,1792]{0,1:T(8,128)(2,1)S(1)} %get-tuple-element.8), kind=kOutput, calls=%fused_computation.1 | convolution fusion | flops 5649989632 | bytes 19005440 | tf_op jit(solution)/shard_map/dot_general | solution.py:42
  144.3 0.0 reduce-scatter.2.cloned.1.call-update
  144.4 0.0 copy-start.6
  144.4 3.4 %copy.15 = f32[384,1792]{1,0:T(8,128)} copy(f32[384,1792]{0,1:T(8,128)} %get-tuple-element.10) | data formatting | bytes 5505024
  147.8 0.0 copy-done.6
  147.8 12.2 %fusion.6 = f32[384,2048]{1,0:T(8,128)} fusion(bf16[2048,3584]{0,1:T(8,128)(2,1)} %all-gather.2.cloned.1.call-done, bf16[384,1792]{0,1:T(8,128)(2,1)} %copy-done.7, bf16[384,1792]{0,1:T(8,128)(2,1)S(1)} %copy-done.6), kind=kOutput, calls=%fused_computation.16 | convolution fusion | flops 5642649600 | bytes 20578304 | tf_op jit(solution)/shard_map/dot_general | solution.py:37
  160.0 109.8 %all-reduce.1 = bf16[384,2048]{1,0:T(8,128)(2,1)} all-reduce(f32[384,2048]{1,0:T(8,128)} %fusion.6), channel_id=1, replica_groups=mesh['dp'=8,'tensor'=4] {'tensor'}, use_global_device_ids=true, to_apply=%region_0.0 | all-reduce | flops 786432 | bytes 4718592 | tf_op jit(solution)/shard_map/psum | solution.py:40
  269.8 0.0 reduce-scatter.2.cloned.1.call-done
  269.8 0.0 copy-start.2
  269.8 1.9 convert_element_type.43
  271.7 0.1 copy-done.2
  271.9 2.3 slice_multiply_fusion.1
  274.2 0.0 copy-start.3
  274.2 0.0 copy-start.1
  274.2 2.9 %copy.17 = f32[256,1792]{1,0:T(8,128)} copy(f32[256,1792]{0,1:T(8,128)} %get-tuple-element.11) | data formatting | bytes 3670016
  277.1 0.0 copy-done.3
  277.1 1.7 copy.16
  278.7 0.0 copy-done.1
Async XLA Ops:
  7.2 108.1 %copy-start = (bf16[384,2048]{1,0:T(8,128)(2,1)S(1)}, bf16[384,2048]{1,0:T(8,128)(2,1)}, u32[]{:S(2)}) copy-start(bf16[384,2048]{1,0:T(8,128)(2,1)} %param.6) | copy-start | bytes 4718596
  7.2 108.0 %all-gather.2.cloned.1.call-start = ((), (), s32[]{:S(2)}) async-start(), calls=%async_computation.1 | async-start | bytes 16515072 | tf_op jit(solution)/shard_map/all_gather | solution.py:24
  30.1 239.7 %reduce-scatter.2.cloned.1.call-start = ((), (), s32[]{:S(2)}) async-start(), calls=%async_computation.2 | async-start | bytes 16515072 | tf_op jit(solution)/shard_map/reduce_scatter | solution.py:41
  115.2 10.9 %copy-start.4 = (bf16[384,1792]{0,1:T(8,128)(2,1)S(1)}, bf16[384,1792]{0,1:T(8,128)(2,1)}, u32[]{:S(2)}) copy-start(bf16[384,1792]{0,1:T(8,128)(2,1)} %copy.14) | copy-start | bytes 4128772
  129.3 1.1 copy-start.5
  129.3 1.5 copy-start.7
  144.4 3.4 %copy-start.6 = (bf16[384,1792]{0,1:T(8,128)(2,1)S(1)}, bf16[384,1792]{0,1:T(8,128)(2,1)}, u32[]{:S(2)}) copy-start(bf16[384,1792]{0,1:T(8,128)(2,1)} %copy-done.5) | copy-start | bytes 4128772
  269.8 2.1 copy-start.2
  274.2 2.9 %copy-start.3 = (f32[256,1792]{0,1:T(8,128)S(1)}, f32[256,1792]{0,1:T(8,128)}, u32[]{:S(2)}) copy-start(f32[256,1792]{0,1:T(8,128)} %get-tuple-element.12) | copy-start | bytes 5505028
  274.2 4.6 %copy-start.1 = (bf16[384,2048]{1,0:T(8,128)(2,1)S(1)}, bf16[384,2048]{1,0:T(8,128)(2,1)}, u32[]{:S(2)}) copy-start(bf16[384,2048]{1,0:T(8,128)(2,1)} %param.6) | copy-start | bytes 4718596
Sparse Core Ops, SparseCore 0:
  30.2 84.9 all-gather.1
  144.5 103.5 reduce-scatter.1
where the time goes:
time: 291 us; the launch traced here: 286 us
  blocking collectives  110 us (38%)
  waiting for transfers between devices  82.4 us (28%)
  matrix products  36.6 us (13%)
  local copies, waits for them, and re-layouts  29.9 us (10%)
  between operations  14.1 us (5%)
  other arithmetic  12.5 us (4%)
    psum x1, blocking collectives, local(): grad_tokens = lax.psum(partial_input, 'tensor').astype(jnp.bfloat16)  110 us
    all_gather x1, waiting for transfers between devices, local(): gathered = lax.all_gather(local_both, 'dp', axis=0, tiled=True)  82.4 us
    unnamed x22, local copies, waits for them, and re-layouts  16.6 us
    dot_general x1, matrix products, local(): lax.dot_general(tokens, d_both, (((0,), (0,)), ((), ())), preferred_eleme...  13.5 us
    dot_general x1, matrix products, local(): lax.dot_general(d_both, gathered, (((1,), (1,)), ((), ())), preferred_ele...  12.2 us
    dot_general x1, matrix products, local(): preact = jnp.dot(tokens, gathered, preferred_element_type=jnp.float32)  10.8 us
    reshape x2, local copies, waits for them, and re-layouts, expand(): jnp.broadcast_to(values[:, None, :, None], (height, BLOCK, breadth, BLOCK))  8.43 us
  transfers between devices with their start and end apart: 2, of which 1 were waited for; matrix products, arithmetic and copies ran while one was open for 6% of the time, Pallas kernels for 0%

commit v1 on v0

v1 whole, which is shorter than its diff:
```python
import functools

import jax
import jax.numpy as jnp
from jax import lax
from jax.experimental import pallas as pl
from jax.experimental.pallas import tpu as pltpu
from jax.sharding import PartitionSpec as P

MESH_ID = pl.DeviceIdType.MESH
F32 = jnp.float32
BF16 = jnp.bfloat16
LEAD = 3


def expand(block_mask, rows, columns):
    height, breadth = block_mask.shape
    down, across = rows // height, columns // breadth
    values = block_mask.astype(F32)
    return jnp.broadcast_to(
        values[:, None, :, None], (height, down, breadth, across)
    ).reshape(rows, columns)


def local_collective(tokens, out_grad, gate_weight, up_weight, gate_mask, up_mask):
    gate_keep = expand(gate_mask, *gate_weight.shape)
    up_keep = expand(up_mask, *up_weight.shape)
    gate_eff = gate_weight * gate_keep.astype(BF16)
    up_eff = up_weight * up_keep.astype(BF16)
    local_both = jnp.concatenate([gate_eff, up_eff], axis=1)
    hidden_width = gate_weight.shape[1]
    gathered = lax.all_gather(local_both, "dp", axis=0, tiled=True)
    preact = jnp.dot(tokens, gathered, preferred_element_type=F32)
    gate = preact[:, :hidden_width]
    up = preact[:, hidden_width:]
    sigmoid_gate = jax.nn.sigmoid(gate)
    activation = gate * sigmoid_gate
    hidden = activation * up
    grad_float = out_grad.astype(F32)
    d_gate = (grad_float * up * sigmoid_gate * (1.0 + gate * (1.0 - sigmoid_gate))).astype(BF16)
    d_up = (grad_float * activation).astype(BF16)
    d_both = jnp.concatenate([d_gate, d_up], axis=1)
    partial_input = lax.dot_general(
        d_both, gathered, (((1,), (1,)), ((), ())), preferred_element_type=F32
    )
    grad_tokens = lax.psum(partial_input, "tensor").astype(BF16)
    summed = lax.psum_scatter(
        lax.dot_general(
            tokens, d_both, (((0,), (0,)), ((), ())), preferred_element_type=F32
        ).astype(BF16),
        "dp",
        scatter_dimension=0,
        tiled=True,
    ).astype(F32)
    grad_gate = summed[:, :hidden_width] * gate_keep
    grad_up = summed[:, hidden_width:] * up_keep
    return (hidden, grad_tokens, grad_gate, grad_up)


def kernel(
    n_t, chunks, width, mask_rows,
    tok, og, gw, uw, gm, um,
    hidden, gt, ggrad, ugrad,
    wbuf, mr, xr, yr, r2, tokt, pre, dch, acc, zs, zr,
    ag_s, ag_r, ms_s, ms_r, rs_s, rs_r, z_s, z_r, za_s, za_r,
):
    rows = gw.shape[0]
    half = rows // 2
    n_tok, depth = tok.shape
    n_dp = depth // rows
    d = lax.axis_index("dp")
    t = lax.axis_index("tensor")
    c = lax.rem(d, 2)
    x = lax.rem(d // 2, 2)
    y = d // 4
    mate = d + 1 - 2 * c
    xn = d + 2 - 4 * x
    yn = d + 4 - 8 * y
    dg = xn + 4 - 8 * y

    barrier = pltpu.get_barrier_semaphore()
    for peer in (mate, xn, yn):
        pl.semaphore_signal(barrier, inc=1, device_id=(peer, t), device_id_type=MESH_ID)
    for k in range(1, n_t):
        pl.semaphore_signal(
            barrier, inc=1, device_id=(d, lax.rem(t + k, n_t)), device_id_type=MESH_ID
        )

    def at(j, block, off=0, size=rows):
        return wbuf.at[j, pl.ds(pl.multiple_of(block * rows + off, half), size)]

    def ag(kind, j):
        block, off, size, dev = (
            (d, 0, rows, xn),
            (d, 0, rows, yn),
            (xn, 0, half, yn),
            (yn, half, half, xn),
            (d, 0, rows, mate),
            (xn, 0, rows, mate),
            (yn, 0, rows, mate),
            (dg, 0, rows, mate),
        )[kind]
        return pltpu.make_async_remote_copy(
            src_ref=at(j, block, off, size), dst_ref=at(j, block, off, size),
            send_sem=ag_s.at[kind, j], recv_sem=ag_r.at[kind, j],
            device_id=(dev, t), device_id_type=MESH_ID,
        )

    def ag_in(kind, j):
        m = mate
        block, off, size = (
            (xn, 0, rows), (yn, 0, rows), (dg, 0, half), (dg, half, half),
            (m, 0, rows), (xn + m - d, 0, rows), (yn + m - d, 0, rows), (dg + m - d, 0, rows),
        )[kind]
        return pltpu.make_async_remote_copy(
            src_ref=at(j, block, off, size), dst_ref=at(j, block, off, size),
            send_sem=ag_s.at[kind, j], recv_sem=ag_r.at[kind, j],
            device_id=(mate, t), device_id_type=MESH_ID,
        )

    def ms(q, j):
        return pltpu.make_async_remote_copy(
            src_ref=at(j, 2 * q + 1 - c), dst_ref=mr.at[j, q],
            send_sem=ms_s.at[q, j], recv_sem=ms_r.at[q, j],
            device_id=(mate, t), device_id_type=MESH_ID,
        )

    def rs(kind, j):
        block, off, dst, dev = (
            (dg, 0, xr.at[j, 1], xn),
            (dg, half, yr.at[j, 1], yn),
            (xn, 0, xr.at[j, 0], xn),
            (yn, half, yr.at[j, 0], yn),
            (yn, 0, r2.at[j, 0], yn),
            (xn, half, r2.at[j, 1], xn),
        )[kind]
        return pltpu.make_async_remote_copy(
            src_ref=at(j, block, off, half), dst_ref=dst,
            send_sem=rs_s.at[kind, j], recv_sem=rs_r.at[kind, j],
            device_id=(dev, t), device_id_type=MESH_ID,
        )

    def cols(j):
        return pl.ds(pl.multiple_of(j * width, width), width)

    def keep(ref, j):
        down = rows // mask_rows
        return jnp.concatenate(
            [jnp.broadcast_to(ref[i:i + 1, cols(j)], (down, width)) for i in range(mask_rows)],
            axis=0,
        )

    def prepare(j):
        own = pl.ds(pl.multiple_of(d * rows, rows), rows)
        wbuf[j, own, :width] = (gw[:, cols(j)].astype(F32) * keep(gm, j)).astype(BF16)
        wbuf[j, own, width:] = (uw[:, cols(j)].astype(F32) * keep(um, j)).astype(BF16)

    def send_own(j):
        ag(0, j).start()
        ag(1, j).start()
        ag(4, j).start()

    lax.fori_loop(0, chunks, lambda j, u: (prepare(j), u)[1], 0)
    pl.semaphore_wait(barrier, 3 + n_t - 1)
    lead = min(LEAD, chunks)
    lax.fori_loop(0, lead, lambda j, u: (send_own(j), u)[1], 0)

    tokt[...] = tok[...].T
    acc[...] = jnp.zeros_like(acc)

    def relay(j):
        ag_in(0, j).wait_recv()
        ag(2, j).start()
        ag(5, j).start()
        ag_in(1, j).wait_recv()
        ag(3, j).start()
        ag(6, j).start()

        @pl.when(j + lead < chunks)
        def _():
            send_own(j + lead)

    def relay_far(j):
        ag_in(2, j).wait_recv()
        ag_in(3, j).wait_recv()
        ag(7, j).start()

    def compute(j):
        for kind in (4, 5, 6, 7):
            ag_in(kind, j).wait_recv()
        pre[...] = jnp.dot(tok[...], wbuf[j], preferred_element_type=F32)
        step = n_tok // 3 if n_tok % 48 == 0 else n_tok
        for i in range(0, n_tok, step):
            part = slice(i, i + step)
            gate = pre[part, :width]
            up = pre[part, width:]
            s = jax.nn.sigmoid(gate)
            activation = gate * s
            hidden[part, cols(j)] = activation * up
            g = og[part, cols(j)].astype(F32)
            dch[part, :width] = (g * up * s * (1.0 + gate * (1.0 - s))).astype(BF16)
            dch[part, width:] = (g * activation).astype(BF16)
        for b in range(n_dp):
            acc[:, b * rows:(b + 1) * rows] += lax.dot_general(
                dch[...], wbuf[j, b * rows:(b + 1) * rows, :],
                (((1,), (1,)), ((), ())), preferred_element_type=F32,
            )
        for kind in range(8):
            ag(kind, j).wait_send()
        for q in range(n_dp // 2):
            other = pl.ds(pl.multiple_of((2 * q + 1 - c) * rows, rows), rows)
            wbuf[j, other] = jnp.dot(
                tokt[other], dch[...], preferred_element_type=F32
            ).astype(BF16)
            ms(q, j).start()
        for q in range(n_dp // 2):
            mine = pl.ds(pl.multiple_of((2 * q + c) * rows, rows), rows)
            wbuf[j, mine] = jnp.dot(
                tokt[mine], dch[...], preferred_element_type=F32
            ).astype(BF16)

    def pair_sum(j):
        for q in range(n_dp // 2):
            mine = pl.ds(pl.multiple_of((2 * q + c) * rows, rows), rows)
            ms(q, j).wait_recv()
            wbuf[j, mine] = (wbuf[j, mine].astype(F32) + mr[j, q].astype(F32)).astype(BF16)
        for kind in range(4):
            rs(kind, j).start()

    def cross_sum(j):
        far = pl.ds(pl.multiple_of(yn * rows, rows), half)
        rs(0, j).wait_recv()
        wbuf[j, far] = (wbuf[j, far].astype(F32) + xr[j, 1].astype(F32)).astype(BF16)
        rs(4, j).start()
        far = pl.ds(pl.multiple_of(xn * rows + half, half), half)
        rs(1, j).wait_recv()
        wbuf[j, far] = (wbuf[j, far].astype(F32) + yr[j, 1].astype(F32)).astype(BF16)
        rs(5, j).start()

    def finish(j):
        for kind in (2, 3, 4, 5):
            rs(kind, j).wait_recv()
        for k, near in ((0, xr), (1, yr)):
            own = pl.ds(pl.multiple_of(d * rows + k * half, half), half)
            total = wbuf[j, own].astype(F32) + near[j, 0].astype(F32) + r2[j, k].astype(F32)
            part = slice(k * half, (k + 1) * half)
            ggrad[part, cols(j)] = total[:, :width] * keep(gm, j)[part]
            ugrad[part, cols(j)] = total[:, width:] * keep(um, j)[part]

    def drain(j):
        for q in range(n_dp // 2):
            ms(q, j).wait_send()
        for kind in range(6):
            rs(kind, j).wait_send()

    def when(stage, j):
        @pl.when(jnp.logical_and(j >= 0, j < chunks))
        def _():
            stage(j)

    def step(s, u):
        when(relay, s)
        when(relay_far, s - 1)
        when(compute, s - 2)
        when(pair_sum, s - 3)
        return u

    lax.fori_loop(0, chunks + 2, step, 0)

    quarter = n_tok // n_t

    def zc(k):
        dev = lax.rem(t + k, n_t)
        return pltpu.make_async_remote_copy(
            src_ref=zs.at[k - 1], dst_ref=zr.at[k - 1],
            send_sem=z_s.at[k - 1], recv_sem=z_r.at[k - 1],
            device_id=(d, dev), device_id_type=MESH_ID,
        )

    def band(q):
        return pl.ds(pl.multiple_of(q * quarter, quarter), quarter)

    def za(k):
        dev = lax.rem(t + k, n_t)
        return pltpu.make_async_remote_copy(
            src_ref=gt.at[band(t)], dst_ref=gt.at[band(t)],
            send_sem=za_s.at[k - 1], recv_sem=za_r.at[k - 1],
            device_id=(d, dev), device_id_type=MESH_ID,
        )

    def za_in(k):
        dev = lax.rem(t + n_t - k, n_t)
        return pltpu.make_async_remote_copy(
            src_ref=gt.at[band(dev)], dst_ref=gt.at[band(dev)],
            send_sem=za_s.at[k - 1], recv_sem=za_r.at[k - 1],
            device_id=(d, dev), device_id_type=MESH_ID,
        )

    for k in range(1, n_t):
        dev = lax.rem(t + k, n_t)
        zs[k - 1] = acc[band(dev)].astype(BF16)
        zc(k).start()
    pair_sum(chunks - 1)
    lax.fori_loop(0, min(4, chunks), lambda j, u: (cross_sum(j), u)[1], 0)

    total = acc[band(t)]
    for k in range(1, n_t):
        zc(k).wait_recv()
        total += zr[k - 1].astype(F32)
    gt[band(t)] = total.astype(BF16)
    for k in range(1, n_t):
        za(k).start()
    lax.fori_loop(min(4, chunks), chunks, lambda j, u: (cross_sum(j), u)[1], 0)
    lax.fori_loop(0, chunks, lambda j, u: (finish(j), u)[1], 0)
    lax.fori_loop(0, chunks, lambda j, u: (drain(j), u)[1], 0)
    for k in range(1, n_t):
        zc(k).wait_send()
        za(k).wait_send()
        za_in(k).wait_recv()


def local_fused(n_dp, n_t, width, tokens, out_grad, gate_weight, up_weight, gate_mask, up_mask):
    n_tok, depth = tokens.shape
    rows, hidden_width = gate_weight.shape
    chunks = hidden_width // width
    half = rows // 2
    mask_rows = gate_mask.shape[0]
    gm = expand(gate_mask, mask_rows, hidden_width)
    um = expand(up_mask, mask_rows, hidden_width)
    vmem = pl.BlockSpec(memory_space=pltpu.VMEM)
    return pl.pallas_call(
        functools.partial(kernel, n_t, chunks, width, mask_rows),
        out_shape=(
            jax.ShapeDtypeStruct((n_tok, hidden_width), F32),
            jax.ShapeDtypeStruct((n_tok, depth), BF16),
            jax.ShapeDtypeStruct((rows, hidden_width), F32),
            jax.ShapeDtypeStruct((rows, hidden_width), F32),
        ),
        in_specs=[vmem] * 6,
        out_specs=(vmem,) * 4,
        scratch_shapes=[
            pltpu.VMEM((chunks, depth, 2 * width), BF16),
            pltpu.VMEM((chunks, n_dp // 2, rows, 2 * width), BF16),
            pltpu.VMEM((chunks, 2, half, 2 * width), BF16),
            pltpu.VMEM((chunks, 2, half, 2 * width), BF16),
            pltpu.VMEM((chunks, 2, half, 2 * width), BF16),
            pltpu.VMEM((depth, n_tok), BF16),
            pltpu.VMEM((n_tok, 2 * width), F32),
            pltpu.VMEM((n_tok, 2 * width), BF16),
            pltpu.VMEM((n_tok, depth), F32),
            pltpu.VMEM((n_t - 1, n_tok // n_t, depth), BF16),
            pltpu.VMEM((n_t - 1, n_tok // n_t, depth), BF16),
            pltpu.SemaphoreType.DMA((8, chunks)),
            pltpu.SemaphoreType.DMA((8, chunks)),
            pltpu.SemaphoreType.DMA((n_dp // 2, chunks)),
            pltpu.SemaphoreType.DMA((n_dp // 2, chunks)),
            pltpu.SemaphoreType.DMA((6, chunks)),
            pltpu.SemaphoreType.DMA((6, chunks)),
            pltpu.SemaphoreType.DMA((n_t - 1,)),
            pltpu.SemaphoreType.DMA((n_t - 1,)),
            pltpu.SemaphoreType.DMA((n_t - 1,)),
            pltpu.SemaphoreType.DMA((n_t - 1,)),
        ],
        compiler_params=pltpu.CompilerParams(
            collective_id=0, has_side_effects=True, vmem_limit_bytes=60 * 1024 * 1024
        ),
        cost_estimate=pl.CostEstimate(
            flops=12 * n_tok * depth * hidden_width,
            bytes_accessed=8 * n_tok * hidden_width,
            transcendentals=n_tok * hidden_width,
        ),
    )(tokens, out_grad, gate_weight, up_weight, gm, um)


def solution(mesh):
    placed = (
        P("dp", None),
        P("dp", "tensor"),
        P("dp", "tensor"),
        P("dp", "tensor"),
        P("dp", "tensor"),
        P("dp", "tensor"),
    )
    n_dp, n_t = mesh.shape["dp"], mesh.shape["tensor"]

    def local(tokens, out_grad, gate_weight, up_weight, gate_mask, up_mask):
        args = (tokens, out_grad, gate_weight, up_weight, gate_mask, up_mask)
        width = 256
        fits = (
            n_dp == 2 ** 3
            and n_t > 1
            and gate_weight.shape[1] % width == 0
            and gate_weight.shape[0] % 256 == 0
            and tokens.shape[0] % (16 * n_t) == 0
        )
        if fits:
            return local_fused(n_dp, n_t, width, *args)
        return local_collective(*args)

    return jax.shard_map(
        local,
        mesh=mesh,
        in_specs=placed,
        out_specs=(P("dp", "tensor"), P("dp", None), P("dp", "tensor"), P("dp", "tensor")),
        check_vma=False,
    )
```

time: 291 us -> 177 us (0.61); the launches traced: 286 us -> 177 us
  Pallas kernels: 0 us -> 164 us
  blocking collectives: 110 us -> 0 us
  waiting for transfers between devices: 82.4 us -> 0 us
  matrix products: 36.6 us -> 0 us
  local copies, waits for them, and re-layouts: 29.9 us -> 10.6 us
  between operations: 14.1 us -> 0.65 us
  other arithmetic: 12.5 us -> 1.37 us
    pallas_call x0 -> x1, Pallas kernels: none -> 164 us  [local_fused(): pl.pallas_call(functools.partial(kernel, n_t, chunks, width, mask_rows),...]
    psum x1 -> x0, blocking collectives: 110 us -> none  [local(): grad_tokens = lax.psum(partial_input, 'tensor').astype(jnp.bfloat16)]
    all_gather x1 -> x0, waiting for transfers between devices: 82.4 us -> none  [local(): gathered = lax.all_gather(local_both, 'dp', axis=0, tiled=True)]
    dot_general x3 -> x0, matrix products: 36.6 us -> none  [the longest x1 13.5 us: local(): lax.dot_general(tokens, d_both, (((0,), (0,)), ((), ())), preferred_eleme...]
    reshape x2 -> x0, local copies, waits for them, and re-layouts: 8.43 us -> none  [expand(): jnp.broadcast_to(values[:, None, :, None], (height, BLOCK, breadth, BLOCK))]
    unnamed x22 -> x10, local copies, waits for them, and re-layouts: 16.6 us -> 9.07 us
    convert_element_type x4 -> x2, other arithmetic: 6.59 us -> 1.37 us  [expand(): values = block_mask.astype(F32)]
    mul x2 -> x0, other arithmetic: 4.59 us -> none  [the longest x1 2.33 us: local(): grad_up = summed[:, hidden_width:] * up_keep]
  transfers between devices with their start and end apart: 2 -> 0, of which waited for: 1 -> 0; matrix products, arithmetic and copies ran while one was open for 6% -> 0% of each run, Pallas kernels for 0% -> 0%
where the time goes in v1:
time: 177 us
  Pallas kernels  164 us (93%)
  local copies, waits for them, and re-layouts  10.6 us (6%)
    pallas_call x1, Pallas kernels, local_fused(): pl.pallas_call(functools.partial(kernel, n_t, chunks, width, mask_rows),...  164 us
    unnamed x10, local copies, waits for them, and re-layouts  9.07 us

profile of v1, /device:TPU:8, one launch (start us, length us, event | category | flops | bytes accessed | tf_op | source)
XLA Modules:
  0.0 177.0 jit_solution(11301793147550097177)
XLA Ops:
  0.6 0.7 convert_element_type.6
  1.3 0.7 convert_element_type.7
  2.0 0.1 broadcast_in_dim.18
  2.1 0.7 broadcast_in_dim.19.um
  2.8 0.1 broadcast_in_dim.16
  2.9 0.7 broadcast_in_dim.17.gm
  3.6 164.3 %shard_map.93 = (f32[384,1792]{1,0:T(8,128)}, bf16[384,2048]{1,0:T(8,128)(2,1)}, f32[256,1792]{1,0:T(8,128)}, f32[256,1792]{1,0:T(8,128)}) custom-call(bf16[384,2048]{1,0:T(8,128)(2,1)} %tok.1, bf16[384,1792]{1,0:T(8,128)(2,1)} %og.1, bf16[256,1792]{1,0:T(8,128)(2,1)} %gw.1, bf16[256,1792]{1,0:T(8,128)(2,1)} %uw.1, f32[4,1792]{1,0:T(4,128)} %broadcast_in_dim.17.gm, ...), custom_call_target="tpu_custom_call" | custom-call | flops 16911433728 | bytes 5505024 | tf_op jit(solution)/shard_map/pallas_call | solution.py:331
  167.9 0.0 copy-start.2
  167.9 3.6 %copy.14 = f32[384,1792]{1,0:T(8,128)} copy(f32[384,1792]{1,0:T(8,128)} %get-tuple-element.8) | data formatting | bytes 5505024
  171.5 0.0 copy-done.2
  171.5 0.0 copy-start.1
  171.5 1.1 copy.15
  172.7 0.9 copy-done.1
  173.6 0.0 copy-start
  173.6 1.2 copy.16
  174.8 0.9 copy-done
  175.8 1.2 copy.17
Async XLA Ops:
  167.9 3.6 %copy-start.2 = (bf16[384,2048]{1,0:T(8,128)(2,1)S(1)}, bf16[384,2048]{1,0:T(8,128)(2,1)}, u32[]{:S(2)}) copy-start(bf16[384,2048]{1,0:T(8,128)(2,1)} %get-tuple-element.9) | copy-start | bytes 4718596
  171.5 2.1 %copy-start.1 = (f32[256,1792]{1,0:T(8,128)S(1)}, f32[256,1792]{1,0:T(8,128)}, u32[]{:S(2)}) copy-start(f32[256,1792]{1,0:T(8,128)} %get-tuple-element.10) | copy-start | bytes 5505028
  173.6 2.2 %copy-start = (f32[256,1792]{1,0:T(8,128)S(1)}, f32[256,1792]{1,0:T(8,128)}, u32[]{:S(2)}) copy-start(f32[256,1792]{1,0:T(8,128)} %get-tuple-element.11) | copy-start | bytes 5505028

commit v2 on v1

--- a/solution.py
+++ b/solution.py
@@ -11,6 +11,7 @@
 F32 = jnp.float32
 BF16 = jnp.bfloat16
 LEAD = 3
+EARLY = 2
 
 
 def expand(block_mask, rows, columns):
@@ -160,10 +161,22 @@
         ag(1, j).start()
         ag(4, j).start()
 
-    lax.fori_loop(0, chunks, lambda j, u: (prepare(j), u)[1], 0)
+    prepare(0)
     pl.semaphore_wait(barrier, 3 + n_t - 1)
     lead = min(LEAD, chunks)
-    lax.fori_loop(0, lead, lambda j, u: (send_own(j), u)[1], 0)
+
+    def begin(j, u):
+        @pl.when(j < lead)
+        def _():
+            send_own(j)
+
+        @pl.when(j + 1 < chunks)
+        def _():
+            prepare(j + 1)
+
+        return u
+
+    lax.fori_loop(0, chunks, begin, 0)
 
     tokt[...] = tok[...].T
     acc[...] = jnp.zeros_like(acc)
@@ -184,6 +197,40 @@
         ag_in(2, j).wait_recv()
         ag_in(3, j).wait_recv()
         ag(7, j).start()
+
+    quarter = n_tok // n_t
+
+    def zc(k):
+        dev = lax.rem(t + k, n_t)
+        return pltpu.make_async_remote_copy(
+            src_ref=zs.at[k - 1], dst_ref=zr.at[k - 1],
+            send_sem=z_s.at[k - 1], recv_sem=z_r.at[k - 1],
+            device_id=(d, dev), device_id_type=MESH_ID,
+        )
+
+    def band(q):
+        return pl.ds(pl.multiple_of(q * quarter, quarter), quarter)
+
+    def za(k):
+        dev = lax.rem(t + k, n_t)
+        return pltpu.make_async_remote_copy(
+            src_ref=gt.at[band(t)], dst_ref=gt.at[band(t)],
+            send_sem=za_s.at[k - 1], recv_sem=za_r.at[k - 1],
+            device_id=(d, dev), device_id_type=MESH_ID,
+        )
+
+    def za_in(k):
+        dev = lax.rem(t + n_t - k, n_t)
+        return pltpu.make_async_remote_copy(
+            src_ref=gt.at[band(dev)], dst_ref=gt.at[band(dev)],
+            send_sem=za_s.at[k - 1], recv_sem=za_r.at[k - 1],
+            device_id=(d, dev), device_id_type=MESH_ID,
+        )
+
+    def send_input_terms():
+        for k in range(1, n_t):
+            zs[k - 1] = acc[band(lax.rem(t + k, n_t))].astype(BF16)
+            zc(k).start()
 
     def compute(j):
         for kind in (4, 5, 6, 7):
@@ -196,7 +243,7 @@
             up = pre[part, width:]
             s = jax.nn.sigmoid(gate)
             activation = gate * s
-            hidden[part, cols(j)] = activation * up
+            hidden[part, cols(j)] = (activation * up).astype(BF16)
             g = og[part, cols(j)].astype(F32)
             dch[part, :width] = (g * up * s * (1.0 + gate * (1.0 - s))).astype(BF16)
             dch[part, width:] = (g * activation).astype(BF16)
@@ -205,6 +252,11 @@
                 dch[...], wbuf[j, b * rows:(b + 1) * rows, :],
                 (((1,), (1,)), ((), ())), preferred_element_type=F32,
             )
+
+        @pl.when(j == chunks - 1)
+        def _():
+            send_input_terms()
+
         for kind in range(8):
             ag(kind, j).wait_send()
         for q in range(n_dp // 2):
@@ -244,8 +296,8 @@
             own = pl.ds(pl.multiple_of(d * rows + k * half, half), half)
             total = wbuf[j, own].astype(F32) + near[j, 0].astype(F32) + r2[j, k].astype(F32)
             part = slice(k * half, (k + 1) * half)
-            ggrad[part, cols(j)] = total[:, :width] * keep(gm, j)[part]
-            ugrad[part, cols(j)] = total[:, width:] * keep(um, j)[part]
+            ggrad[part, cols(j)] = (total[:, :width] * keep(gm, j)[part]).astype(BF16)
+            ugrad[part, cols(j)] = (total[:, width:] * keep(um, j)[part]).astype(BF16)
 
     def drain(j):
         for q in range(n_dp // 2):
@@ -262,47 +314,20 @@
         when(relay, s)
         when(relay_far, s - 1)
         when(compute, s - 2)
-        when(pair_sum, s - 3)
+        when(pair_sum, s - 6)
         return u
 
     lax.fori_loop(0, chunks + 2, step, 0)
 
-    quarter = n_tok // n_t
-
-    def zc(k):
-        dev = lax.rem(t + k, n_t)
-        return pltpu.make_async_remote_copy(
-            src_ref=zs.at[k - 1], dst_ref=zr.at[k - 1],
-            send_sem=z_s.at[k - 1], recv_sem=z_r.at[k - 1],
-            device_id=(d, dev), device_id_type=MESH_ID,
-        )
-
-    def band(q):
-        return pl.ds(pl.multiple_of(q * quarter, quarter), quarter)
-
-    def za(k):
-        dev = lax.rem(t + k, n_t)
-        return pltpu.make_async_remote_copy(
-            src_ref=gt.at[band(t)], dst_ref=gt.at[band(t)],
-            send_sem=za_s.at[k - 1], recv_sem=za_r.at[k - 1],
-            device_id=(d, dev), device_id_type=MESH_ID,
-        )
-
-    def za_in(k):
-        dev = lax.rem(t + n_t - k, n_t)
-        return pltpu.make_async_remote_copy(
-            src_ref=gt.at[band(dev)], dst_ref=gt.at[band(dev)],
-            send_sem=za_s.at[k - 1], recv_sem=za_r.at[k - 1],
-            device_id=(d, dev), device_id_type=MESH_ID,
-        )
-
-    for k in range(1, n_t):
-        dev = lax.rem(t + k, n_t)
-        zs[k - 1] = acc[band(dev)].astype(BF16)
-        zc(k).start()
-    pair_sum(chunks - 1)
-    lax.fori_loop(0, min(4, chunks), lambda j, u: (cross_sum(j), u)[1], 0)
-
+    lax.fori_loop(max(0, chunks - 4), chunks, lambda j, u: (pair_sum(j), u)[1], 0)
+
+    def settle(j, u):
+        when(cross_sum, j)
+        when(finish, j - 2)
+        return u
+
+    early = min(EARLY, chunks)
+    lax.fori_loop(0, early, settle, 0)
     total = acc[band(t)]
     for k in range(1, n_t):
         zc(k).wait_recv()
@@ -310,8 +335,7 @@
     gt[band(t)] = total.astype(BF16)
     for k in range(1, n_t):
         za(k).start()
-    lax.fori_loop(min(4, chunks), chunks, lambda j, u: (cross_sum(j), u)[1], 0)
-    lax.fori_loop(0, chunks, lambda j, u: (finish(j), u)[1], 0)
+    lax.fori_loop(early, chunks + 2, settle, 0)
     lax.fori_loop(0, chunks, lambda j, u: (drain(j), u)[1], 0)
     for k in range(1, n_t):
         zc(k).wait_send()
@@ -328,13 +352,13 @@
     gm = expand(gate_mask, mask_rows, hidden_width)
     um = expand(up_mask, mask_rows, hidden_width)
     vmem = pl.BlockSpec(memory_space=pltpu.VMEM)
-    return pl.pallas_call(
+    hidden, grad_tokens, grad_gate, grad_up = pl.pallas_call(
         functools.partial(kernel, n_t, chunks, width, mask_rows),
         out_shape=(
-            jax.ShapeDtypeStruct((n_tok, hidden_width), F32),
+            jax.ShapeDtypeStruct((n_tok, hidden_width), BF16),
             jax.ShapeDtypeStruct((n_tok, depth), BF16),
-            jax.ShapeDtypeStruct((rows, hidden_width), F32),
-            jax.ShapeDtypeStruct((rows, hidden_width), F32),
+            jax.ShapeDtypeStruct((rows, hidden_width), BF16),
+            jax.ShapeDtypeStruct((rows, hidden_width), BF16),
         ),
         in_specs=[vmem] * 6,
         out_specs=(vmem,) * 4,
@@ -370,6 +394,7 @@
             transcendentals=n_tok * hidden_width,
         ),
     )(tokens, out_grad, gate_weight, up_weight, gm, um)
+    return hidden.astype(F32), grad_tokens, grad_gate.astype(F32), grad_up.astype(F32)
 
 
 def solution(mesh):

time: 177 us -> 159 us (0.90)
  Pallas kernels: 164 us -> 147 us
  local copies, waits for them, and re-layouts: 10.6 us -> 3.6 us
  other arithmetic: 1.37 us -> 7.2 us
    pallas_call x1, Pallas kernels: 164 us -> 147 us  [local_fused(): pl.pallas_call(functools.partial(kernel, n_t, chunks, width, mask_rows),...]
    unnamed x10 -> x7, local copies, waits for them, and re-layouts: 9.07 us -> 2.03 us
    convert_element_type x0 -> x3, other arithmetic: none -> 5.83 us  [the longest x1 3.13 us: local_fused(): hidden.astype(F32)]
where the time goes in v2:
time: 159 us
  Pallas kernels  147 us (92%)
  other arithmetic  7.2 us (5%)
  local copies, waits for them, and re-layouts  3.6 us (2%)
    pallas_call x1, Pallas kernels, local_fused(): pl.pallas_call(functools.partial(kernel, n_t, chunks, width, mask_rows),...  147 us

profile of v2, /device:TPU:8, one launch (start us, length us, event | category | flops | bytes accessed | tf_op | source)
XLA Modules:
  0.0 158.8 jit_solution(16395363109261356250)
XLA Ops:
  0.6 0.7 convert_element_type.15
  1.3 0.7 convert_element_type.16
  2.0 0.1 broadcast_in_dim.18
  2.1 0.7 broadcast_in_dim.19.um
  2.8 0.1 broadcast_in_dim.16
  2.9 0.7 broadcast_in_dim.17.gm
  3.6 147.4 %shard_map.93 = (bf16[384,1792]{1,0:T(8,128)(2,1)}, bf16[384,2048]{1,0:T(8,128)(2,1)}, bf16[256,1792]{1,0:T(8,128)(2,1)}, bf16[256,1792]{1,0:T(8,128)(2,1)}) custom-call(bf16[384,2048]{1,0:T(8,128)(2,1)} %tok.1, bf16[384,1792]{1,0:T(8,128)(2,1)} %og.1, bf16[256,1792]{1,0:T(8,128)(2,1)} %gw.1, bf16[256,1792]{1,0:T(8,128)(2,1)} %uw.1, ...), custom_call_target="tpu_custom_call" | custom-call | flops 16911433728 | bytes 5505024 | tf_op jit(solution)/shard_map/pallas_call | solution.py:355
  151.0 0.0 copy-start.2
  151.0 3.1 %convert_element_type.17 = f32[384,1792]{1,0:T(8,128)} convert(bf16[384,1792]{1,0:T(8,128)(2,1)} %get-tuple-element.8) | non-fusion elementwise | flops 688128 | bytes 4128768 | tf_op jit(solution)/shard_map/convert_element_type | solution.py:397
  154.1 0.0 copy-done.2
  154.1 0.0 copy-start.1
  154.1 1.3 convert_element_type.18
  155.5 0.2 copy-done.1
  155.6 0.0 copy-start
  155.6 1.3 convert_element_type.19
  157.0 0.7 copy-done
  157.7 1.1 copy.11
Async XLA Ops:
  151.0 3.1 %copy-start.2 = (bf16[256,1792]{1,0:T(8,128)(2,1)S(1)}, bf16[256,1792]{1,0:T(8,128)(2,1)}, u32[]{:S(2)}) copy-start(bf16[256,1792]{1,0:T(8,128)(2,1)} %get-tuple-element.10) | copy-start | bytes 2752516
  154.1 1.5 copy-start.1
  155.6 2.1 %copy-start = (bf16[384,2048]{1,0:T(8,128)(2,1)S(1)}, bf16[384,2048]{1,0:T(8,128)(2,1)}, u32[]{:S(2)}) copy-start(bf16[384,2048]{1,0:T(8,128)(2,1)} %get-tuple-element.17) | copy-start | bytes 4718596

commit v3 on v2

--- a/solution.py
+++ b/solution.py
@@ -10,14 +10,14 @@
 MESH_ID = pl.DeviceIdType.MESH
 F32 = jnp.float32
 BF16 = jnp.bfloat16
-LEAD = 3
+LEAD = 2
 EARLY = 2
 
 
-def expand(block_mask, rows, columns):
+def expand(block_mask, rows, columns, kind=F32):
     height, breadth = block_mask.shape
     down, across = rows // height, columns // breadth
-    values = block_mask.astype(F32)
+    values = block_mask.astype(kind)
     return jnp.broadcast_to(
         values[:, None, :, None], (height, down, breadth, across)
     ).reshape(rows, columns)
@@ -147,7 +147,10 @@
     def keep(ref, j):
         down = rows // mask_rows
         return jnp.concatenate(
-            [jnp.broadcast_to(ref[i:i + 1, cols(j)], (down, width)) for i in range(mask_rows)],
+            [
+                jnp.broadcast_to(ref[i:i + 1, cols(j)].astype(F32), (down, width))
+                for i in range(mask_rows)
+            ],
             axis=0,
         )
 
@@ -349,8 +352,8 @@
     chunks = hidden_width // width
     half = rows // 2
     mask_rows = gate_mask.shape[0]
-    gm = expand(gate_mask, mask_rows, hidden_width)
-    um = expand(up_mask, mask_rows, hidden_width)
+    gm = expand(gate_mask, mask_rows, hidden_width, jnp.int32)
+    um = expand(up_mask, mask_rows, hidden_width, jnp.int32)
     vmem = pl.BlockSpec(memory_space=pltpu.VMEM)
     hidden, grad_tokens, grad_gate, grad_up = pl.pallas_call(
         functools.partial(kernel, n_t, chunks, width, mask_rows),

time: 159 us -> 158 us (level)
  no operation moved by 1% of the time
where the time goes in v3:
time: 158 us; the launch traced here: 157 us
  Pallas kernels  146 us (92%)
  other arithmetic  5.83 us (4%)
  local copies, waits for them, and re-layouts  4.96 us (3%)
    pallas_call x1, Pallas kernels, local_fused(): pl.pallas_call(functools.partial(kernel, n_t, chunks, width, mask_rows),...  146 us

profile of v3, /device:TPU:8, one launch (start us, length us, event | category | flops | bytes accessed | tf_op | source)
XLA Modules:
  0.0 157.5 jit_solution(1395534020325209057)
XLA Ops:
  0.6 0.8 broadcast_in_dim.16
  1.4 0.7 broadcast_in_dim.17.gm
  2.1 0.8 broadcast_in_dim.18
  2.9 0.7 broadcast_in_dim.19.um
  3.6 146.0 %shard_map.93 = (bf16[384,1792]{1,0:T(8,128)(2,1)}, bf16[384,2048]{1,0:T(8,128)(2,1)}, bf16[256,1792]{1,0:T(8,128)(2,1)}, bf16[256,1792]{1,0:T(8,128)(2,1)}) custom-call(bf16[384,2048]{1,0:T(8,128)(2,1)} %tok.1, bf16[384,1792]{1,0:T(8,128)(2,1)} %og.1, bf16[256,1792]{1,0:T(8,128)(2,1)} %gw.1, bf16[256,1792]{1,0:T(8,128)(2,1)} %uw.1, ...), custom_call_target="tpu_custom_call" | custom-call | flops 16911433728 | bytes 5505024 | tf_op jit(solution)/shard_map/pallas_call | solution.py:358
  149.6 0.0 copy-start.2
  149.6 3.1 %convert_element_type.9 = f32[384,1792]{1,0:T(8,128)} convert(bf16[384,1792]{1,0:T(8,128)(2,1)} %get-tuple-element.8) | non-fusion elementwise | flops 688128 | bytes 4128768 | tf_op jit(solution)/shard_map/convert_element_type | solution.py:400
  152.7 0.0 copy-done.2
  152.7 0.0 copy-start.1
  152.7 1.3 convert_element_type.10
  154.1 0.2 copy-done.1
  154.2 0.0 copy-start
  154.2 1.3 convert_element_type.11
  155.6 0.7 copy-done
  156.3 1.1 copy.11
Async XLA Ops:
  149.6 3.1 %copy-start.2 = (bf16[256,1792]{1,0:T(8,128)(2,1)S(1)}, bf16[256,1792]{1,0:T(8,128)(2,1)}, u32[]{:S(2)}) copy-start(bf16[256,1792]{1,0:T(8,128)(2,1)} %get-tuple-element.10) | copy-start | bytes 2752516
  152.7 1.5 copy-start.1
  154.2 2.1 %copy-start = (bf16[384,2048]{1,0:T(8,128)(2,1)S(1)}, bf16[384,2048]{1,0:T(8,128)(2,1)}, u32[]{:S(2)}) copy-start(bf16[384,2048]{1,0:T(8,128)(2,1)} %get-tuple-element.17) | copy-start | bytes 4718596
